TPU v7x, 256 devices: a whole 4x4x8 slice. The times are simulated.
256 devices in a mesh: dp: 4 (over x), ctx: 16 (over y_hi, z), tensor: 4 (over y_lo, core).
Axes of the slice: x: 4, y: 4 (y_hi: 2, y_lo: 2; y = y_hi * 2 + y_lo), z: 8, core: 2. Of those that a mesh axis runs over, the one named last changes fastest.
Arguments:
- residues: bfloat16 [8192, 2560], P(('dp', 'ctx')), parts along dimension 0, may hold values from -6 to 6
- chain_ids: int32 [8192], P(('dp', 'ctx')), parts along dimension 0, may hold values from 0 to 3, never falling along the last dimension, each value on 1 to 1024 neighbouring positions
- residue_valid: int32 [8192], P(('dp', 'ctx')), parts along dimension 0, may hold values from 0 to 1, as said below
- layer_weights: bfloat16 [4, 2560, 1536], P(None, 'ctx', 'tensor')
- resampler_weights: bfloat16 [4, 2560, 1536], P(None, 'ctx', 'tensor')
- norm_gains: float32 [3, 2560], replicated, may hold values from 0.25 to 1.75
- norm_biases: float32 [3, 2560], replicated, may hold values from -2 to 2
- latents: bfloat16 [128, 2560], replicated, may hold values from -6 to 6
Outputs:
- hidden_states: bfloat16 [8192, 2560], P(('dp', 'ctx'), 'tensor'), parts along dimension 0
- latent_out: bfloat16 [512, 2560], P(('dp', 'ctx'), 'tensor'), parts along dimension 0
There are 4 independent parts, one for each index of `dp`. A program takes and returns all parts, laid end to end along the dimension named above; an argument that names none is the same for every part. Nothing has to cross between parts.
Inputs may be any that keep to these rules, and one draw needn't show every extreme that they name: `chain_ids`: ids never fall along the group; 4 chains of 1 to 1024 residues, one of exactly 1024. `residue_valid`: the group's first residue is always 1.
All inputs are finite; a program needn't handle non-finite values.
Results may differ from a plain program's by a relative error of at most 0.034.
The roundings to bfloat16 on the way count: a program that leaves them out, or rounds other values in their place, can miss the bound.
Values may be sent and summed in bfloat16 or wider, within the bound.
A program may use at most 64 MiB of HBM per device.

v0:
```python
import math

import jax
import jax.numpy as jnp
from jax import lax
from jax.sharding import PartitionSpec as P

HDIM = 64


NEGATIVE = -1e30
EPSILON = 1e-05


def combined_all(value, axis, join):
    pieces = jax.tree.map(lambda part: lax.all_gather(part, axis), value)
    head = jax.tree.map(lambda part: part[0], pieces)
    tail = jax.tree.map(lambda part: part[1:], pieces)
    total, _ = lax.scan(lambda total, piece: (join(total, piece), None), head, tail)
    return total


def layer_norm(matrix, gain_row, bias_row):
    as_float = matrix.astype(jnp.float32)
    average = jnp.mean(as_float, axis=-1, keepdims=True)
    centred = as_float - average
    variance = jnp.mean(centred * centred, axis=-1, keepdims=True)
    return centred * lax.rsqrt(variance + EPSILON) * gain_row + bias_row


def rotary(matrix, positions, head_dim):
    row_count = matrix.shape[0]
    per_head = matrix.reshape(row_count, -1, head_dim)
    half_dim = head_dim // 2
    frequency = jnp.exp(
        jnp.arange(half_dim, dtype=jnp.float32) * (-2.0 * math.log(10000.0) / head_dim)
    )
    angles = positions.astype(jnp.float32)[:, None] * frequency[None, :]
    cos_part = jnp.cos(angles)[:, None, :]
    sin_part = jnp.sin(angles)[:, None, :]
    lower_half = per_head[..., :half_dim]
    upper_half = per_head[..., half_dim:]
    turned = jnp.concatenate(
        [
            lower_half * cos_part - upper_half * sin_part,
            upper_half * cos_part + lower_half * sin_part,
        ],
        axis=-1,
    )
    return turned.reshape(row_count, -1)


def contract_last(left, right):
    return lax.dot_general(
        left, right, (((1,), (1,)), ((), ())), preferred_element_type=jnp.float32
    )


def per_device(
    residues,
    chain_ids,
    residue_valid,
    layer_weights,
    resampler_weights,
    norm_gains,
    norm_biases,
    latents,
):
    tok_rows = residues.shape[0]
    model_width = residues.shape[1]
    inner_local = layer_weights.shape[2]
    head_count = inner_local // HDIM
    ctx_size = lax.axis_size("ctx")
    tensor_size = lax.axis_size("tensor")
    ctx_rank = lax.axis_index("ctx")
    tensor_rank = lax.axis_index("tensor")
    col_width = model_width // tensor_size
    col_start = tensor_rank * col_width
    q_scale = HDIM ** (-0.5)
    positions = ctx_rank * tok_rows + jnp.arange(tok_rows, dtype=jnp.int32)
    normed = layer_norm(residues, norm_gains[0], norm_biases[0]).astype(jnp.bfloat16)
    layer_full, resampler_full = (
        lax.all_gather(layer_weights, "ctx", axis=1, tiled=True),
        lax.all_gather(resampler_weights, "ctx", axis=1, tiled=True),
    )
    query_raw = jnp.dot(normed, layer_full[0], preferred_element_type=jnp.float32)
    key_raw = jnp.dot(normed, layer_full[1], preferred_element_type=jnp.float32)
    value_raw = jnp.dot(normed, layer_full[2], preferred_element_type=jnp.float32)
    queries = rotary(query_raw * q_scale, positions, HDIM).astype(jnp.bfloat16)
    key_rows = rotary(key_raw, positions, HDIM).astype(jnp.bfloat16)
    value_rows = value_raw.astype(jnp.bfloat16)
    key_tags = jnp.where(residue_valid > 0, chain_ids, -1).astype(jnp.bfloat16)
    query_heads = queries.reshape(tok_rows, head_count, HDIM)
    own_chain = chain_ids.astype(jnp.float32)
    start_state = (
        jnp.full((head_count, tok_rows), NEGATIVE, jnp.float32),
        jnp.zeros((head_count, tok_rows), jnp.float32),
        jnp.zeros((head_count, tok_rows, HDIM), jnp.float32),
    )
    part_keys = lax.all_gather(key_rows, "ctx", axis=0, tiled=True)
    part_values = lax.all_gather(value_rows, "ctx", axis=0, tiled=True)
    part_tags = lax.all_gather(key_tags, "ctx", axis=0, tiled=True)
    piece_rows = part_keys.shape[0]
    block_size = math.gcd(piece_rows, 512)

    def one_block(block_index, running_state):
        maximum, totals, numerator = running_state
        first_row = block_index * block_size
        block_keys = lax.dynamic_slice_in_dim(part_keys, first_row, block_size, 0).reshape(
            block_size, head_count, HDIM
        )
        block_values = lax.dynamic_slice_in_dim(part_values, first_row, block_size, 0).reshape(
            block_size, head_count, HDIM
        )
        block_tags = lax.dynamic_slice_in_dim(part_tags, first_row, block_size, 0).astype(
            jnp.float32
        )
        key_pos = first_row + jnp.arange(block_size, dtype=jnp.int32)
        allowed = (own_chain[:, None] == block_tags[None, :]) | (
            positions[:, None] == key_pos[None, :]
        )
        scores = jnp.einsum(
            "qhd,khd->hqk", query_heads, block_keys, preferred_element_type=jnp.float32
        )
        scores = jnp.where(allowed[None], scores, NEGATIVE)
        new_max = jnp.maximum(maximum, jnp.max(scores, axis=2))
        rescale = jnp.exp(maximum - new_max)
        unrounded = jnp.where(allowed[None], jnp.exp(scores - new_max[:, :, None]), 0.0)
        totals = totals * rescale + jnp.sum(unrounded, axis=2)
        numerator = numerator * rescale[:, :, None] + jnp.einsum(
            "hqk,khd->hqd",
            unrounded.astype(jnp.bfloat16),
            block_values,
            preferred_element_type=jnp.float32,
        )
        return (new_max, totals, numerator)

    maximum, totals, numerator = lax.fori_loop(0, piece_rows // block_size, one_block, start_state)
    attended = (
        (numerator / totals[:, :, None])
        .transpose(1, 0, 2)
        .reshape(tok_rows, inner_local)
        .astype(jnp.bfloat16)
    )
    head_terms = contract_last(attended, layer_full[3])
    summed = lax.psum(head_terms, "tensor")
    updated = residues.astype(jnp.float32) + summed
    hidden_out = lax.dynamic_slice_in_dim(updated, col_start, col_width, 1).astype(jnp.bfloat16)
    residue_normed = layer_norm(updated, norm_gains[1], norm_biases[1]).astype(jnp.bfloat16)
    latent_normed = layer_norm(latents, norm_gains[2], norm_biases[2]).astype(jnp.bfloat16)
    latent_count = latents.shape[0]
    latent_raw = jnp.dot(latent_normed, resampler_full[0], preferred_element_type=jnp.float32)
    res_key_raw = jnp.dot(residue_normed, resampler_full[1], preferred_element_type=jnp.float32)
    res_value_raw = jnp.dot(residue_normed, resampler_full[2], preferred_element_type=jnp.float32)
    latent_query = (
        (latent_raw * q_scale).astype(jnp.bfloat16).reshape(latent_count, head_count, HDIM)
    )
    residue_key = res_key_raw.astype(jnp.bfloat16).reshape(tok_rows, head_count, HDIM)
    residue_value = res_value_raw.astype(jnp.bfloat16).reshape(tok_rows, head_count, HDIM)
    usable = residue_valid > 0
    lat_scores = jnp.einsum(
        "lhd,khd->hlk", latent_query, residue_key, preferred_element_type=jnp.float32
    )
    lat_scores = jnp.where(usable[None, None, :], lat_scores, NEGATIVE)
    lat_max = jnp.max(lat_scores, axis=2)
    lat_unrounded = jnp.where(usable[None, None, :], jnp.exp(lat_scores - lat_max[:, :, None]), 0.0)
    lat_totals = jnp.sum(lat_unrounded, axis=2)
    lat_numerator = jnp.einsum(
        "hlk,khd->hld",
        lat_unrounded.astype(jnp.bfloat16),
        residue_value,
        preferred_element_type=jnp.float32,
    )
    latent_rows = latent_count // ctx_size
    own_start = ctx_rank * latent_rows

    def combine(former, latter):
        max_former, tot_former, num_former = former
        max_latter, tot_latter, num_latter = latter
        joined = jnp.maximum(max_former, max_latter)
        scale_former = jnp.exp(max_former - joined)
        scale_latter = jnp.exp(max_latter - joined)
        return (
            joined,
            tot_former * scale_former + tot_latter * scale_latter,
            num_former * scale_former[:, :, None] + num_latter * scale_latter[:, :, None],
        )

    merged_max, merged_totals, merged_numerator = combined_all(
        (lat_max, lat_totals, lat_numerator), "ctx", combine
    )
    own_totals = lax.dynamic_slice_in_dim(merged_totals, own_start, latent_rows, 1)
    own_numerator = lax.dynamic_slice_in_dim(merged_numerator, own_start, latent_rows, 1)
    latent_attended = (
        (own_numerator / own_totals[:, :, None])
        .transpose(1, 0, 2)
        .reshape(latent_rows, inner_local)
        .astype(jnp.bfloat16)
    )
    latent_terms = contract_last(latent_attended, resampler_full[3])
    latent_share = lax.psum_scatter(
        latent_terms.astype(jnp.bfloat16), "tensor", scatter_dimension=1, tiled=True
    ).astype(jnp.float32)
    own_latents = lax.dynamic_slice_in_dim(
        lax.dynamic_slice_in_dim(latents, own_start, latent_rows, 0), col_start, col_width, 1
    )
    latent_out = (own_latents.astype(jnp.float32) + latent_share).astype(jnp.bfloat16)
    return (hidden_out, latent_out)


def solution(mesh):
    placed = (
        P(("dp", "ctx"), None),
        P(("dp", "ctx")),
        P(("dp", "ctx")),
        P(None, "ctx", "tensor"),
        P(None, "ctx", "tensor"),
        P(),
        P(),
        P(),
    )
    return jax.shard_map(
        per_device,
        mesh=mesh,
        in_specs=placed,
        out_specs=(P(("dp", "ctx"), "tensor"), P(("dp", "ctx"), "tensor")),
        check_vma=False,
    )
```

profile of v0, /device:TPU:1, one launch (start us, length us, event | category | flops | bytes accessed | tf_op | source)
XLA Modules:
  0.0 652.9 jit_solution(1465094083343678025)
XLA Ops:
  7.2 0.7 all-gather.12.cloned.1.call-update
  8.0 1.1 slice_reduce_fusion
  9.1 1.3 convert_reduce_fusion
  10.9 133.9 %all-gather.12.cloned.1.call-done = bf16[4,2560,384]{2,1,0:T(8,128)(2,1)} async-done(((bf16[4,160,384]{2,1,0:T(8,128)(2,1)}), bf16[4,2560,384]{2,1,0:T(8,128)(2,1)}) %all-gather.12.cloned.1.call-update) | async-done | bytes 7864336 | tf_op jit(solution)/shard_map/all_gather | solution.py:83
  144.8 2.1 fusion.31
  147.0 1.7 slice_bitcast_fusion.14
  148.8 2.4 copy.32
  151.2 2.3 fusion.38
  153.6 0.6 pad_maximum_fusion
  154.3 2.7 fusion.34
  157.2 0.5 all-gather.18.cloned.1.call-update
  157.8 29.4 %all-gather.3 = bf16[16,1,128]{2,1,0:T(2,128)(2,1)S(1)} all-gather(bf16[1,1,128]{2,1,0:T(2,128)(2,1)S(1)} %get-tuple-element.359), channel_id=1, replica_groups=mesh['dp'=4,'ctx'=16,'tensor'=4] {'ctx'}, dimensions={0}, use_global_device_ids=true | all-gather | bytes 4352 | tf_op jit(solution)/shard_map/all_gather | solution.py:102
  187.3 41.5 %all-gather.14.cloned.1.call-done = bf16[2048,384]{0,1:T(8,128)(2,1)} async-done(((bf16[128,384]{0,1:T(8,128)(2,1)}), bf16[2048,384]{0,1:T(8,128)(2,1)}) %all-gather.14.cloned.1.call-update) | async-done | bytes 1572880 | tf_op jit(solution)/shard_map/all_gather | solution.py:100
  228.8 80.9 %all-gather.16.cloned.1.call-done = bf16[2048,384]{1,0:T(8,128)(2,1)} async-done(((bf16[128,384]{1,0:T(8,128)(2,1)}), bf16[2048,384]{1,0:T(8,128)(2,1)}) %all-gather.16.cloned.1.call-update) | async-done | bytes 1572880 | tf_op jit(solution)/shard_map/all_gather | solution.py:101
  309.7 15.4 %while.33 = (s32[]{:T(128)}, f32[6,128]{1,0:T(8,128)S(1)}, f32[6,128]{1,0:T(8,128)S(1)}, f32[6,128,64]{1,2,0:T(8,128)S(1)}, f32[128]{0:T(128)S(1)}, /*index=5*/b...) while((s32[]{:T(128)}, f32[6,128]{1,0:T(8,128)S(1)}, ...), condition=%wide.region_5.6_spmd.clone, body=%wide.region_2.5_spmd.clone.sunk | while | flops 104158080 | bytes 8678107 | solution.py:138
  309.7 1.0 constant_dynamic-slice_fusion.8
  311.8 1.0 constant_dynamic-slice_fusion.9
  313.1 0.4 convolution_add_fusion.2
  313.6 1.0 constant_dynamic-slice_fusion.8
  314.9 0.4 fusion.84
  315.7 1.0 constant_dynamic-slice_fusion.9
  316.9 0.4 convolution_add_fusion.2
  317.4 1.0 constant_dynamic-slice_fusion.8
  318.8 0.4 fusion.84
  319.5 1.0 constant_dynamic-slice_fusion.9
  321.3 1.0 constant_dynamic-slice_fusion.8
  323.4 1.1 constant_dynamic-slice_fusion.9
  324.7 0.4 convolution_add_fusion.2
  325.2 3.4 fusion.16
  328.7 1.0 copy-done.1
  330.2 112.5 %all-gather.18.cloned.1.call-done = bf16[4,2560,384]{2,1,0:T(8,128)(2,1)} async-done(((bf16[4,160,384]{2,1,0:T(8,128)(2,1)}), bf16[4,2560,384]{2,1,0:T(8,128)(2,1)}) %all-gather.18.cloned.1.call-update) | async-done | bytes 7864336 | tf_op jit(solution)/shard_map/all_gather | solution.py:84
  442.7 2.1 fusion.33
  445.0 47.6 %all-reduce.2.cloned.1.call-done = f32[128,2560]{1,0:T(8,128)} async-done(((f32[128,2560]{1,0:T(8,128)}), f32[128,2560]{1,0:T(8,128)}) %all-reduce.2.cloned.1.call-update) | async-done | bytes 1310736 | tf_op jit(solution)/shard_map/psum | solution.py:146
  492.6 1.5 fusion.57
  494.4 2.1 fusion.35
  496.7 2.1 fusion.36
  499.2 1.0 fusion.46
  500.2 34.1 %all-gather.4 = f32[16,6,128]{2,1,0:T(8,128)S(1)} all-gather(f32[1,6,128]{2,1,0:T(8,128)S(1)} %bitcast.117), channel_id=2, replica_groups=mesh['dp'=4,'ctx'=16,'tensor'=4] {'ctx'}, dimensions={0}, use_global_device_ids=true | all-gather | bytes 52224 | tf_op jit(solution)/shard_map/all_gather | solution.py:16
  534.5 29.2 %all-gather.5 = f32[16,6,128]{2,1,0:T(8,128)S(1)} all-gather(f32[1,6,128]{2,1,0:T(8,128)S(1)} %bitcast.119), channel_id=3, replica_groups=mesh['dp'=4,'ctx'=16,'tensor'=4] {'ctx'}, dimensions={0}, use_global_device_ids=true | all-gather | bytes 52224 | tf_op jit(solution)/shard_map/all_gather | solution.py:16
  563.7 27.3 %all-gather.20.cloned.1.call-done = f32[96,128,64]{1,2,0:T(8,128)} async-done(((f32[6,128,64]{1,2,0:T(8,128)}), f32[96,128,64]{1,2,0:T(8,128)}) %all-gather.20.cloned.1.call-update) | async-done | bytes 3145744 | tf_op jit(solution)/shard_map/all_gather | solution.py:16
  591.0 0.9 slice.119
  592.1 3.9 slice.122
  596.1 22.9 %while.32 = (s32[]{:T(128)}, f32[6,128]{1,0:T(8,128)S(1)}, f32[6,128]{1,0:T(8,128)S(1)}, f32[6,128,64]{2,1,0:T(8,128)S(1)}, f32[15,6,128]{2,1,0:T(8,128)S(1)}, /...) while((s32[]{:T(128)}, f32[6,128]{1,0:T(8,128)S(1)}, f32[6,128]{1,0:T(8,128)S(1)}, ...), condition=%wide.region_14.15_spmd, body=%wide.region_13.14_spmd.sunk | while | flops 152066 | bytes 1407077 | solution.py:19
  596.1 0.9 constant_dynamic-slice_fusion.7
  597.6 0.9 constant_dynamic-slice_fusion.7
  599.1 0.9 constant_dynamic-slice_fusion.7
  600.7 0.9 constant_dynamic-slice_fusion.7
  602.2 0.9 constant_dynamic-slice_fusion.7
  603.7 0.9 constant_dynamic-slice_fusion.7
  605.2 0.9 constant_dynamic-slice_fusion.7
  606.8 0.9 constant_dynamic-slice_fusion.7
  608.3 0.9 constant_dynamic-slice_fusion.7
  609.8 0.9 constant_dynamic-slice_fusion.7
  611.4 0.9 constant_dynamic-slice_fusion.7
  612.9 0.9 constant_dynamic-slice_fusion.7
  614.4 0.9 constant_dynamic-slice_fusion.7
  615.9 0.9 constant_dynamic-slice_fusion.7
  617.5 0.9 constant_dynamic-slice_fusion.7
  619.2 2.1 convolution_convert_fusion
  621.4 1.1 copy.44
  622.5 0.7 dynamic-slice_convert_fusion.1
  623.2 21.2 %reduce-scatter.4.cloned.1.call-done = bf16[640,8]{1,0:T(8,128)(2,1)} async-done(((bf16[2560,8]{1,0:T(8,128)(2,1)}), bf16[640,8]{1,0:T(8,128)(2,1)}) %reduce-scatter.4.cloned.1.call-update) | async-done | bytes 10256
  644.4 1.0 copy.45
  645.4 0.7 add_convert_fusion.3
  (140 shorter events, 15.9 us)
Async XLA Ops:
  7.2 3.2 copy-start
  7.2 137.6 %all-gather.12.cloned.1.call-start = ((), (), s32[]{:S(2)}) async-start(), calls=%async_computation.1 | async-start | bytes 8355840 | tf_op jit(solution)/shard_map/all_gather | solution.py:83
  7.9 220.9 %all-gather.14.cloned.1.call-start = ((), (), s32[]{:S(2)}) async-start(), calls=%async_computation.2 | async-start | bytes 1671168 | tf_op jit(solution)/shard_map/all_gather | solution.py:100
  154.3 3.5 copy-start.2
  154.3 3.5 copy-start.3
  154.3 155.4 %all-gather.16.cloned.1.call-start = ((), (), s32[]{:S(2)}) async-start(), calls=%async_computation.3 | async-start | bytes 1671168 | tf_op jit(solution)/shard_map/all_gather | solution.py:101
  157.1 285.6 %all-gather.18.cloned.1.call-start = ((), (), s32[]{:S(2)}) async-start(), calls=%async_computation.5 | async-start | bytes 8355840 | tf_op jit(solution)/shard_map/all_gather | solution.py:84
  157.7 334.9 %all-reduce.2.cloned.1.call-start = ((), (), s32[]{:S(2)}) async-start(), calls=%async_computation.4 | async-start | bytes 2621440 | tf_op jit(solution)/shard_map/psum | solution.py:146
  328.6 1.1 copy-start.1
  328.6 262.4 %all-gather.20.cloned.1.call-start = ((), (), s32[]{:S(2)}) async-start(), calls=%async_computation.6 | async-start | bytes 3342336 | tf_op jit(solution)/shard_map/all_gather | solution.py:16
  500.2 144.2 %reduce-scatter.4.cloned.1.call-start = ((), (), s32[]{:S(2)}) async-start(), calls=%async_computation.7 | async-start | bytes 819200
Sparse Core Ops, SparseCore 0:
  10.6 134.1 all-gather.11
  154.4 74.3 all-gather.13
  231.4 78.2 all-gather.15
  312.2 130.5 all-gather.17
  445.2 47.2 all-reduce.1
  500.3 90.6 all-gather.19
  622.6 21.6 reduce-scatter.3
where the time goes:
time: 654 us; the launch traced here: 653 us
  waiting for transfers between devices  466 us (71%)
  blocking collectives  92.8 us (14%)
  local copies, waits for them, and re-layouts  40.7 us (6%)
  matrix products  23.8 us (4%)
  between operations  14.4 us (2%)
  other arithmetic  13.9 us (2%)
    all_gather x1, waiting for transfers between devices, per_device(): lax.all_gather(layer_weights, 'ctx', axis=1, tiled=True)  134 us
    all_gather x1, waiting for transfers between devices, per_device(): lax.all_gather(resampler_weights, 'ctx', axis=1, tiled=True)  113 us
    all_gather x1, waiting for transfers between devices, per_device(): part_values = lax.all_gather(value_rows, 'ctx', axis=0, tiled=True)  80.9 us
    all_gather x2, blocking collectives, combined_all(): pieces = jax.tree.map(lambda part: lax.all_gather(part, axis), value)  63.3 us
    psum x1, waiting for transfers between devices, per_device(): summed = lax.psum(head_terms, 'tensor')  47.6 us
    all_gather x1, waiting for transfers between devices, per_device(): part_keys = lax.all_gather(key_rows, 'ctx', axis=0, tiled=True)  41.5 us
    all_gather x1, blocking collectives, per_device(): part_tags = lax.all_gather(key_tags, 'ctx', axis=0, tiled=True)  29.4 us
    all_gather x1, waiting for transfers between devices, combined_all(): pieces = jax.tree.map(lambda part: lax.all_gather(part, axis), value)  27.3 us
  transfers between devices with their start and end apart: 7, of which 7 were waited for; matrix products, arithmetic and copies ran while one was open for 4% of the time, Pallas kernels for 0%

commit v1 on v0

v1 whole, which is shorter than its diff:
```python
import functools
import math

import jax
import jax.numpy as jnp
import numpy as np
from jax import lax
from jax.experimental import pallas as pl
from jax.experimental.pallas import tpu as pltpu
from jax.sharding import PartitionSpec as P

HDIM = 64
NEGATIVE = -1e30
EPSILON = 1e-05
ROWS = 128
COLS = 384
WIDTH = 2560
DEPTH = 160
HALF = 80
CUT = 48
SLICE = 640
BLOCKS = 16
RING = 8
MESH = pl.DeviceIdType.MESH
F32 = jnp.float32
BF16 = jnp.bfloat16


def angle_tables():
    half = HDIM // 2
    freq = np.exp(np.arange(half, dtype=np.float32) * np.float32(-2.0 * math.log(10000.0) / HDIM))
    lanes = np.tile(np.concatenate([freq, freq]), COLS // HDIM).astype(np.float64)
    inner = np.arange(ROWS)[:, None] * lanes[None, :]
    outer = (np.arange(BLOCKS) * ROWS)[:, None] * lanes[None, :]
    return [t.astype(np.float32) for t in (np.cos(inner), np.sin(inner), np.cos(outer), np.sin(outer))]


def normalised(x, gain, bias):
    average = jnp.mean(x, axis=-1, keepdims=True)
    centred = x - average
    variance = jnp.mean(centred * centred, axis=-1, keepdims=True)
    return centred * lax.rsqrt(variance + EPSILON) * gain + bias


def contract_last(left, right):
    return lax.dot_general(left, right, (((1,), (1,)), ((), ())), preferred_element_type=F32)


def pair_stack(pair):
    lane = lax.broadcasted_iota(jnp.int32, pair.shape, 1)
    wide = pair.astype(F32)
    first = jnp.where(lane < HDIM, wide, 0.0)
    second = jnp.where(lane < HDIM, 0.0, wide)
    return jnp.concatenate([first, second], axis=0).astype(BF16)


def kernel(
    res_ref, chain_ref, valid_ref, lw_ref, rw_ref, gain_hbm, bias_hbm, lat_hbm, ci_hbm, si_hbm, co_hbm, so_hbm,
    hid_ref, out_ref,
    wb, xb, chain_row, valid_row, gain_ref, bias_ref, lat_ref, ci_ref, si_ref, co_ref, so_ref,
    kvb, att, hb, ho, rn, lq, rkv, pk, rb, lp, lb, lat32, fin,
    load_s, perm_s, perm_r, ring_s, ring_r, x_s, x_r, xx_s, xx_r, sib_s, sib_r,
    kv_s, kv_r, kvs_s, kvs_r, rs_s, rs_r, ag_s, ag_r, ho_s, ho_r, a2_s, a2_r, lo_s, lo_r,
):
    x = lax.axis_index("dp")
    ctx = lax.axis_index("ctx")
    ten = lax.axis_index("tensor")
    y_hi, z = lax.div(ctx, 8), lax.rem(ctx, 8)
    y_lo, core = lax.div(ten, 2), lax.rem(ten, 2)
    r = core * 8 + z
    group = y_lo * 2 + y_hi
    native = y_hi == core
    moved = y_hi != core

    def dev(yh, yl, zz, cc, xx=x):
        return (xx, yh * 8 + zz, yl * 2 + cc)

    def zpos(shift):
        return lax.rem(z + (shift % 8), 8)

    right = dev(y_hi, y_lo, zpos(1), core)
    left = dev(y_hi, y_lo, zpos(-1), core)
    sibling = dev(y_hi, y_lo, z, 1 - core)
    partner = dev(1 - y_hi, y_lo, z, 1 - core)
    z_hi, z_lo = lax.div(z, 4), lax.rem(z, 4)
    out_to = dev(z_hi, y_hi, core * 4 + z_lo, y_lo)
    out_from = dev(y_lo, core, y_hi * 4 + z_lo, z_hi)
    out_stays = (y_hi == y_lo) & (y_lo == core) & (core == z_hi)
    out_moves = jnp.logical_not(out_stays)
    opposite = dev(1 - y_hi, 1 - y_lo, z, core)
    x_up = dev(y_hi, y_lo, z, core, lax.rem(x + 1, 4))
    x_down = dev(y_hi, y_lo, z, core, lax.rem(x + 3, 4))

    def peer(offset):
        return lax.rem(group + offset, 4)

    def group_device(g):
        return dev(lax.rem(g, 2), lax.div(g, 2), z, core)

    barrier = pltpu.get_barrier_semaphore()
    greeted = [right, left, sibling, partner, x_up, x_down, out_from] + [group_device(peer(k)) for k in range(1, 4)]
    for device in greeted:
        pl.semaphore_signal(barrier, inc=1, device_id=device, device_id_type=MESH)
    loads = [
        pltpu.make_async_copy(src, dst, load_s.at[k])
        for k, (src, dst) in enumerate(
            [
                (gain_hbm, gain_ref), (bias_hbm, bias_ref), (lat_hbm, lat_ref), (ci_hbm, ci_ref),
                (si_hbm, si_ref), (co_hbm, co_ref), (so_hbm, so_ref),
            ]
        )
    ]
    for load in loads:
        load.start()
    pl.semaphore_wait(barrier, len(greeted))

    def remote(src, dst, ss, rr, device):
        return pltpu.make_async_remote_copy(
            src_ref=src, dst_ref=dst, send_sem=ss, recv_sem=rr, device_id=device, device_id_type=MESH
        )

    def arrived(ref, rr):
        remote(ref, ref, load_s.at[0], rr, sibling).wait_recv()

    def begin(copy):
        copy.start()

    def sent(ref, ss):
        remote(ref, ref, ss, load_s.at[0], sibling).wait_send()

    half = lax.rem(x, 2)

    def piece_z(index):
        step = (index + 1) // 2
        return zpos(-step if index % 2 else step)

    def area(mat, mats, owner, index, offset, rows):
        start = (owner * 8 + piece_z(index)) * DEPTH + offset
        return wb.at[pl.ds(mat, mats), pl.ds(pl.multiple_of(start, 16), rows), :]

    x_moves = [
        (res_ref, xb, 0), (chain_ref, chain_row, 1), (valid_ref, valid_row, 2),
    ]

    def x_copy(k):
        src, dst, sem = x_moves[k]
        return remote(src, dst, perm_s.at[sem], perm_r.at[sem], opposite)

    def x_local(k):
        src, dst, sem = x_moves[k]
        return pltpu.make_async_copy(src, dst, perm_r.at[sem])

    class Chunk:
        def __init__(self, number, source, first, second, quarter):
            self.number, self.mat, self.quarter = number, 2 * number, quarter
            self.source, self.pair = source, (first, second)
            self.x_done = self.xx_done = self.sib_done = 0

        def own(self, offset=0, rows=HALF):
            if self.quarter:
                return self.mat + lax.div(x, 2), 1, half * HALF + offset, rows
            return self.mat, 2, half * HALF + offset, rows

        def of_plane(self, plane, offset=0, rows=HALF):
            plane = lax.rem(plane, 4)
            return self.mat + lax.div(plane, 2), 1, lax.rem(plane, 2) * HALF + offset, rows

        def at(self, owner, index, what):
            mat, mats, offset, rows = what
            return area(mat, mats, owner, index, offset, rows)

        def moves(self):
            rows = pl.ds(pl.multiple_of(half * HALF, 16), HALF)
            first, second = self.pair
            sem = 3 + 2 * self.number
            if self.quarter:
                src = self.source.at[pl.ds(first + (second - first) * lax.div(x, 2), 1), rows, :]
                return [(src, self.own(), sem)]
            if second == first + 1:
                return [(self.source.at[pl.ds(first, 2), rows, :], self.own(), sem)]
            return [
                (self.source.at[pl.ds(m, 1), rows, :], (self.mat + k, 1, half * HALF, HALF), sem + k)
                for k, m in enumerate(self.pair)
                if (self.number, k) != (1, 1)
            ]

        def perm_copies(self):
            out = []
            for src, what, sem in self.moves():
                mat, mats, offset, rows = what
                start = (y_hi * 8 + z) * DEPTH + offset
                there = wb.at[pl.ds(mat, mats), pl.ds(pl.multiple_of(start, 16), rows), :]
                out.append(remote(src, there, perm_s.at[sem], perm_r.at[sem], partner))
            return out

        def perm_start(self):
            @pl.when(native)
            def _():
                for src, what, sem in self.moves():
                    pltpu.make_async_copy(src, self.at(core, 0, what), perm_r.at[sem]).start()

            @pl.when(moved)
            def _():
                for copy in self.perm_copies():
                    copy.start()

        def perm_wait(self):
            @pl.when(native)
            def _():
                for src, what, sem in self.moves():
                    pltpu.make_async_copy(src, self.at(core, 0, what), perm_r.at[sem]).wait()

            @pl.when(moved)
            def _():
                for src, what, sem in self.moves():
                    arrived(self.at(core, 0, what), perm_r.at[sem])

        def ring_copy(self, index, arriving, what, sem):
            ref = self.at(core, index, what)
            target = right if arriving % 2 else left
            return remote(ref, ref, ring_s.at[self.number], ring_r.at[self.number, sem], target)

        def last(self, way):
            if self.quarter:
                return self.own(*((0, CUT), (CUT, HALF - CUT))[way])
            return self.mat + way, 1, half * HALF, HALF

        def x_out(self, side):
            if self.quarter:
                return self.own()
            return self.mat + side, 1, half * HALF, HALF

        def xx_rows(self, side):
            return ((0, CUT), (CUT, HALF - CUT))[side]

        def spread(self, index):
            if index == 0:
                begin(self.ring_copy(0, 1, self.own(), 1))
                begin(self.ring_copy(0, 2, self.own(), 2))
            elif index <= 4:
                begin(self.ring_copy(index, index + 2, self.own(), index + 2))
            elif index <= 6:
                begin(self.ring_copy(index, index, self.last(index - 5), 7))
            if not self.quarter:
                self.sib_start(index, half * HALF, HALF)
            for side in range(2):
                ref = self.at(core, index, self.x_out(side))
                begin(remote(ref, ref, x_s.at[self.number], x_r.at[self.number, index], (x_up, x_down)[side]))

        def ring_wait(self, index):
            arrived(self.at(core, index, self.own()), ring_r.at[self.number, index])

        def x_next(self):
            index = self.x_done
            self.x_done += 1
            arrived(self.at(core, index, (self.mat, 2, 0, HALF)), x_r.at[self.number, index])
            if self.quarter:
                for side in range(2):
                    ref = self.at(core, index, self.of_plane(x + (3, 1)[side], *self.xx_rows(side)))
                    begin(remote(ref, ref, xx_s, xx_r.at[index], (x_up, x_down)[side]))
            else:
                self.sib_start(index, (1 - half) * HALF, HALF)

        def xx_next(self):
            index = self.xx_done
            self.xx_done += 1
            arrived(self.at(core, index, (self.mat, 1, 0, HALF)), xx_r.at[index])
            self.sib_start(index)

        def sib_start(self, index, offset=0, rows=DEPTH):
            ref = self.at(core, index, (self.mat, 2, offset, rows))
            begin(remote(ref, ref, sib_s.at[self.number], sib_r.at[self.number], sibling))

        def step(self, number):
            if number == 0:
                self.spread(0)
                return
            for index in (2 * number - 1, 2 * number):
                if index <= 7:
                    self.ring_wait(index)
                    self.spread(index)
            while self.x_done < 2 * number - 1:
                self.x_next()
            while self.quarter and self.xx_done < 2 * number - 3:
                self.xx_next()

        def finish(self):
            while self.x_done < 8:
                self.x_next()
            while self.quarter and self.xx_done < 8:
                self.xx_next()
            rows = pl.ds(pl.multiple_of((1 - core) * 8 * DEPTH, 16), 8 * DEPTH)
            arrived(wb.at[pl.ds(self.mat, 2), rows, :], sib_r.at[self.number])

        def all_sent(self):
            mats = 1 if self.quarter else 2
            sent(wb.at[pl.ds(0, mats), pl.ds(0, 7 * HALF), :], ring_s.at[self.number])
            sent(wb.at[pl.ds(0, 1), pl.ds(0, 16 * HALF), :], x_s.at[self.number])
            sent(wb.at[pl.ds(0, 2), pl.ds(0, 8 * DEPTH), :], sib_s.at[self.number])
            if self.quarter:
                sent(wb.at[pl.ds(0, 1), pl.ds(0, 8 * HALF), :], xx_s)

    def out_move(block):
        rows = pl.ds(pl.multiple_of(half * HALF, 16), HALF)
        there = pl.ds(pl.multiple_of(block * DEPTH + half * HALF, 16), HALF)
        return lw_ref.at[pl.ds(3, 1), rows, :], wb.at[pl.ds(3, 1), there, :]

    def out_local():
        return pltpu.make_async_copy(*out_move(r), perm_r.at[11])

    def out_remote():
        return remote(*out_move(y_lo * 8 + core * 4 + z_lo), perm_s.at[11], perm_r.at[11], out_to)

    def out_start():
        @pl.when(out_stays)
        def _():
            out_local().start()

        @pl.when(out_moves)
        def _():
            out_remote().start()

    def out_wait():
        @pl.when(out_stays)
        def _():
            out_local().wait()

        @pl.when(out_moves)
        def _():
            arrived(out_move(r)[1], perm_r.at[11])

    keyval = Chunk(0, lw_ref, 1, 2, False)
    query_out = Chunk(1, lw_ref, 0, 3, False)
    res_kv = Chunk(2, rw_ref, 1, 2, True)
    res_qo = Chunk(3, rw_ref, 0, 3, False)
    W_KEY, W_VALUE, W_QUERY, W_OUT, R_KEY, R_VALUE, R_QUERY, R_OUT = range(8)

    keyval.perm_start()
    query_out.perm_start()
    out_start()
    for load in loads:
        load.wait()
    cos_o, sin_o = co_ref[pl.ds(r, 1), :], so_ref[pl.ds(r, 1), :]
    cos_part = ci_ref[...] * cos_o - si_ref[...] * sin_o
    sin_part = si_ref[...] * cos_o + ci_ref[...] * sin_o
    lat_normed = normalised(lat_ref[...].astype(F32), gain_ref[2:3, :], bias_ref[2:3, :]).astype(BF16)
    lat_cols = pl.ds(pl.multiple_of(ten * SLICE, 128), SLICE)
    lat32[...] = lat_ref[:, lat_cols].astype(F32)
    keyval.perm_wait()
    keyval.step(0)
    res_kv.perm_start()
    res_qo.perm_start()

    @pl.when(native)
    def _():
        for k in range(3):
            x_copy(k).start()
            x_local(k).start()

    keyval.step(1)
    query_out.perm_wait()
    out_wait()
    query_out.step(0)
    keyval.step(2)
    query_out.step(1)

    @pl.when(native)
    def _():
        for k in range(3):
            x_local(k).wait()

    @pl.when(moved)
    def _():
        for k in range(3):
            x_copy(k).wait_recv()

    keyval.step(3)
    query_out.step(2)
    keyval.step(4)
    query_out.step(3)
    normed = normalised(xb[...].astype(F32), gain_ref[0:1, :], bias_ref[0:1, :]).astype(BF16)
    keyval.finish()
    res_kv.perm_wait()
    res_kv.step(0)

    lane = lax.broadcasted_iota(jnp.int32, (ROWS, COLS), 1)
    low = lax.rem(lane, HDIM) < HDIM // 2

    def turn(a):
        swapped = jnp.where(
            low, -pltpu.roll(a, COLS - HDIM // 2, 1), pltpu.roll(a, HDIM // 2, 1)
        )
        return a * cos_part + swapped * sin_part

    def project(rows, matrix):
        return jnp.dot(rows, wb[matrix], preferred_element_type=F32)

    K_PART, V_PART = pl.ds(0, ROWS + 16), pl.ds(ROWS + 16, ROWS)

    def kv_start(index, part):
        rows = (K_PART, V_PART)[part]
        if index == 0:
            hops = [(1, 1), (2, 2)]
        elif index <= 4:
            hops = [(index + 2, index + 2)]
        elif index == 5 and part == 0:
            hops = [(7, 7)]
        elif index == 6 and part == 1:
            hops = [(7, 8)]
        else:
            hops = []
        for arriving, way in hops:
            src, dst = kvb.at[2 * index, rows, :], kvb.at[2 * arriving, rows, :]
            target = right if way % 2 else left
            begin(remote(src, dst, kv_s, kv_r.at[part, arriving], target))

    def kv_wait(index, part):
        arrived(kvb.at[2 * index, (K_PART, V_PART)[part], :], kv_r.at[part, index])

    def kv_sib_start(index):
        begin(remote(kvb.at[2 * index], kvb.at[2 * index + 1], kvs_s, kvs_r.at[index], sibling))

    def kv_sib_wait(index):
        arrived(kvb.at[2 * index + 1], kvs_r.at[index])

    def kv_step(number):
        for part in range(2):
            for index in (2 * number - 1, 2 * number):
                if index <= 7:
                    kv_wait(index, part)
                    kv_start(index, part)
        for index in (2 * number - 1, 2 * number):
            if index <= 7:
                kv_sib_start(index)

    chains = chain_row[...].astype(F32)
    valid = valid_row[...] > 0
    key_tag = jnp.where(valid, chains, -1.0)
    kvb[0, 0:ROWS, :] = turn(project(normed, W_KEY)).astype(BF16)
    kvb[0, ROWS : ROWS + 16, :] = jnp.broadcast_to(jnp.concatenate([key_tag] * 3, axis=1), (16, COLS)).astype(BF16)
    kv_start(0, 0)
    kvb[0, ROWS + 16 :, :] = project(normed, W_VALUE).astype(BF16)
    kv_start(0, 1)
    kv_sib_start(0)
    query_out.step(4)
    res_kv.step(1)
    query_out.finish()
    queries = turn(project(normed, W_QUERY) * (HDIM ** -0.5)).astype(BF16)
    stacked = [pair_stack(queries[:, p * 128 : (p + 1) * 128]) for p in range(3)]

    row_at = lax.broadcasted_iota(jnp.int32, (ROWS, ROWS), 0)
    col_at = lax.broadcasted_iota(jnp.int32, (ROWS, ROWS), 1)
    eye = row_at == col_at
    own_chain = jnp.sum(jnp.where(eye, jnp.broadcast_to(chains, (ROWS, ROWS)), 0.0), axis=1, keepdims=True)
    state = [None] * 3

    def attend(first, last):
        count = last - first
        pieces = []
        for slot in range(first, last):
            tag = kvb[slot, ROWS : ROWS + 16, 0:ROWS].astype(F32)[0:1, :]
            allowed = own_chain == tag
            if slot == 0:
                allowed = allowed | eye
            pieces.append(jnp.where(allowed, 0.0, NEGATIVE))
        bias = jnp.concatenate(pieces, axis=1)
        bias = jnp.concatenate([bias, bias], axis=0)
        for pair in range(3):
            cols = slice(pair * 128, (pair + 1) * 128)
            keys = kvb[first:last, 0:ROWS, cols].reshape(count * ROWS, 128)
            values = kvb[first:last, ROWS + 16 :, cols].reshape(count * ROWS, 128)
            scores = contract_last(stacked[pair], keys) + bias
            top = jnp.max(scores, axis=1, keepdims=True)
            if state[pair] is not None:
                top = jnp.maximum(top, state[pair][0])
            unrounded = jnp.exp(scores - top)
            totals = jnp.sum(unrounded, axis=1, keepdims=True)
            mixed = jnp.dot(unrounded.astype(BF16), values, preferred_element_type=F32)
            if state[pair] is not None:
                before, former, numerator = state[pair]
                scale = jnp.exp(before - top)
                totals = totals + former * scale
                mixed = mixed + numerator * scale
            state[pair] = top, totals, mixed

    kv_step(1)
    res_kv.step(2)
    kv_sib_wait(0)
    attend(0, 2)
    kv_step(2)
    res_kv.step(3)
    for index in (1, 2):
        kv_sib_wait(index)
    attend(2, 6)
    kv_step(3)
    res_kv.step(4)
    res_qo.perm_wait()
    res_qo.step(0)
    for index in (3, 4):
        kv_sib_wait(index)
    attend(6, 10)
    kv_step(4)
    for index in (5, 6):
        kv_sib_wait(index)
    attend(10, 14)
    res_qo.step(1)
    kv_sib_wait(7)
    attend(14, 16)
    pair_lane = lax.broadcasted_iota(jnp.int32, (ROWS, ROWS), 1)
    for pair in range(3):
        top, totals, mixed = state[pair]
        mixed = mixed / totals
        cols = slice(pair * 128, (pair + 1) * 128)
        att[group, :, cols] = jnp.where(pair_lane < HDIM, mixed[0:ROWS], mixed[ROWS:]).astype(BF16)

    parts = [pl.ds(0, ROWS // 2), pl.ds(ROWS // 2, ROWS // 2)]
    for h, rows in enumerate(parts):
        for offset in range(1, 4):
            ref = att.at[group, rows, :]
            begin(remote(ref, ref, rs_s, rs_r.at[h, offset], group_device(peer(offset))))
    res_kv.finish()
    res_qo.step(2)
    own_cols = pl.ds(pl.multiple_of(group * SLICE, 128), SLICE)

    def head_terms(g, rows):
        out_rows = pl.ds(pl.multiple_of(g * SLICE, 128), SLICE)
        return contract_last(att[g, rows, :], wb[W_OUT, out_rows, :])

    for h, rows in enumerate(parts):
        updated = xb[rows, own_cols].astype(F32) + head_terms(group, rows)
        for offset in range(1, 4):
            source = peer(4 - offset)
            arrived(att.at[source, rows, :], rs_r.at[h, offset])
            updated = updated + head_terms(source, rows)
        hb[group, rows, :] = updated.astype(BF16)
        for offset in range(1, 4):
            ref = hb.at[group, rows, :]
            begin(remote(ref, ref, ag_s, ag_r.at[h, offset], group_device(peer(offset))))
    res_qo.step(3)
    res_qo.step(4)
    for h, rows in enumerate(parts):
        for offset in range(1, 4):
            arrived(hb.at[peer(4 - offset), rows, :], ag_r.at[h, offset])
        whole = [hb[part, rows, :].astype(F32) for part in range(4)]
        average = sum(jnp.sum(w, axis=1, keepdims=True) for w in whole) / WIDTH
        centred = [w - average for w in whole]
        variance = sum(jnp.sum(c * c, axis=1, keepdims=True) for c in centred) / WIDTH
        scale = lax.rsqrt(variance + EPSILON)
        for part in range(4):
            cols = slice(part * SLICE, (part + 1) * SLICE)
            rn[rows, cols] = (centred[part] * scale * gain_ref[1:2, cols] + bias_ref[1:2, cols]).astype(BF16)

    def to_sibling():
        return remote(hb.at[y_lo * 2 + 1 - core], ho, ho_s, ho_r, sibling)

    def hidden_out(src):
        return pltpu.make_async_copy(src, hid_ref, load_s.at[1])

    @pl.when(native)
    def _():
        to_sibling().start()
        hidden_out(hb.at[group]).start()

    residue_normed = rn[...]
    rkv[0] = project(residue_normed, R_KEY).astype(BF16)
    rkv[1] = project(residue_normed, R_VALUE).astype(BF16)
    res_qo.finish()
    lq[...] = (project(lat_normed, R_QUERY) * (HDIM ** -0.5)).astype(BF16)

    usable = jnp.broadcast_to(valid, (2 * ROWS, ROWS))
    packed = jnp.zeros((ROWS, 128), F32)
    parts = []
    for pair in range(3):
        cols = slice(pair * 128, (pair + 1) * 128)
        scores = contract_last(pair_stack(lq[:, cols]), rkv[0, :, cols])
        scores = jnp.where(usable, scores, NEGATIVE)
        top = jnp.max(scores, axis=1, keepdims=True).astype(BF16).astype(F32)
        unrounded = jnp.where(usable, jnp.exp(scores - top), 0.0)
        totals = jnp.sum(unrounded, axis=1, keepdims=True)
        high = totals.astype(BF16).astype(F32)
        mixed = jnp.dot(unrounded.astype(BF16), rkv[1, :, cols], preferred_element_type=F32)
        parts.append(jnp.where(pair_lane < HDIM, mixed[0:ROWS], mixed[ROWS:]))
        for which in range(2):
            part = slice(which * ROWS, (which + 1) * ROWS)
            head = 2 * pair + which
            packed = jnp.where(pair_lane == head, top[part], packed)
            packed = jnp.where(pair_lane == 16 + head, high[part], packed)
            packed = jnp.where(pair_lane == 32 + head, (totals - high)[part], packed)
    parts.append(packed)
    pk[...] = jnp.concatenate([p.reshape(BLOCKS, 8, 128) for p in parts], axis=1).astype(BF16)

    @pl.when(moved)
    def _():
        arrived(ho, ho_r)
        hidden_out(ho).start()

    def block_rows(block):
        return pl.ds(pl.multiple_of(block * 8, 8), 8)

    for offset in range(1, 16):
        to = lax.rem(r + offset, 16)
        device = dev(y_hi, y_lo, lax.rem(to, 8), lax.div(to, 8))
        begin(remote(pk.at[to], rb.at[r], a2_s, a2_r, device))
    rb[r] = pk[r]
    arrived(rb.at[0:15], a2_r)

    received = rb[...].astype(F32)
    stats = received[:, 24:32, :]
    small_lane = lax.broadcasted_iota(jnp.int32, (BLOCKS, 8, 128), 2)
    pieces = []
    for pair in range(3):
        def spread(first_lane):
            return jnp.where(
                small_lane < HDIM,
                stats[:, :, first_lane : first_lane + 1],
                stats[:, :, first_lane + 1 : first_lane + 2],
            )

        tops = spread(2 * pair)
        weight = jnp.exp(tops - jnp.max(tops, axis=0, keepdims=True))
        total = jnp.sum((spread(16 + 2 * pair) + spread(32 + 2 * pair)) * weight, axis=0)
        mixed = jnp.sum(received[:, 8 * pair : 8 * pair + 8, :] * weight, axis=0)
        pieces.append(mixed / total)
    merged = jnp.concatenate(pieces, axis=1)
    merged = jnp.concatenate([merged, merged], axis=0).astype(BF16)
    for part in range(4):
        lp[part] = contract_last(merged, wb[R_OUT, part * SLICE : (part + 1) * SLICE, :])[0:8]

    def out_copy(part):
        owner = (x, r, jnp.int32(part))
        return remote(lp.at[part], lb.at[group], lo_s.at[part], lo_r.at[group], owner)

    for part in range(4):
        mine = native & (ten == part)

        @pl.when(mine)
        def _():
            lb[group] = lp[part]

        @pl.when(jnp.logical_not(mine))
        def _():
            out_copy(part).start()

    for chunk in (keyval, query_out, res_kv, res_qo):
        chunk.all_sent()
    sent(kvb.at[0:7], kv_s)
    sent(kvb.at[0:8], kvs_s)
    sent(att.at[0:3], rs_s)
    sent(hb.at[0:3], ag_s)
    sent(rb.at[0:15], a2_s)

    @pl.when(native)
    def _():
        for k in range(3):
            x_copy(k).wait_send()
        to_sibling().wait_send()
        hidden_out(hb.at[group]).wait()

    @pl.when(moved)
    def _():
        for chunk in (keyval, query_out, res_kv, res_qo):
            for copy in chunk.perm_copies():
                copy.wait_send()
        hidden_out(ho).wait()

    @pl.when(out_moves)
    def _():
        out_remote().wait_send()

    for part in range(4):
        mine = native & (group == part)

        @pl.when(jnp.logical_not(mine))
        def _():
            arrived(lb.at[part], lo_r.at[part])

    total = lat32[block_rows(ctx), :]
    for part in range(4):
        total = total + lb[part]
    fin[...] = total.astype(BF16)
    last = pltpu.make_async_copy(fin, out_ref, load_s.at[0])
    last.start()
    for part in range(4):
        mine = native & (ten == part)

        @pl.when(jnp.logical_not(mine))
        def _():
            out_copy(part).wait_send()
    last.wait()


def per_device(
    residues, chain_ids, residue_valid, layer_weights, resampler_weights, norm_gains, norm_biases, latents
):
    tables = [jnp.asarray(t) for t in angle_tables()]
    hbm = pl.BlockSpec(memory_space=pl.ANY)
    dma = pltpu.SemaphoreType.DMA
    return pl.pallas_call(
        kernel,
        out_shape=(
            jax.ShapeDtypeStruct((ROWS, SLICE), BF16),
            jax.ShapeDtypeStruct((8, SLICE), BF16),
        ),
        in_specs=[hbm] * 12,
        out_specs=(hbm, hbm),
        scratch_shapes=[
            pltpu.VMEM((8, WIDTH, COLS), BF16),
            pltpu.VMEM((ROWS, WIDTH), BF16),
            pltpu.VMEM((1, ROWS), jnp.int32),
            pltpu.VMEM((1, ROWS), jnp.int32),
            pltpu.VMEM((3, WIDTH), F32),
            pltpu.VMEM((3, WIDTH), F32),
            pltpu.VMEM((ROWS, WIDTH), BF16),
            pltpu.VMEM((ROWS, COLS), F32),
            pltpu.VMEM((ROWS, COLS), F32),
            pltpu.VMEM((BLOCKS, COLS), F32),
            pltpu.VMEM((BLOCKS, COLS), F32),
            pltpu.VMEM((BLOCKS, 2 * ROWS + 16, COLS), BF16),
            pltpu.VMEM((4, ROWS, COLS), BF16),
            pltpu.VMEM((4, ROWS, SLICE), BF16),
            pltpu.VMEM((ROWS, SLICE), BF16),
            pltpu.VMEM((ROWS, WIDTH), BF16),
            pltpu.VMEM((ROWS, COLS), BF16),
            pltpu.VMEM((2, ROWS, COLS), BF16),
            pltpu.VMEM((BLOCKS, 32, 128), BF16),
            pltpu.VMEM((BLOCKS, 32, 128), BF16),
            pltpu.VMEM((4, 8, SLICE), F32),
            pltpu.VMEM((4, 8, SLICE), F32),
            pltpu.VMEM((ROWS, SLICE), F32),
            pltpu.VMEM((8, SLICE), BF16),
            dma((7,)),
            dma((12,)), dma((12,)),
            dma((4,)), dma((4, 8)),
            dma((4,)), dma((4, 8)),
            dma, dma((8,)),
            dma((4,)), dma((4,)),
            dma, dma((2, 8)),
            dma, dma((8,)),
            dma, dma((2, 4)),
            dma, dma((2, 4)),
            dma, dma,
            dma, dma,
            dma((4,)), dma((4,)),
        ],
        compiler_params=pltpu.CompilerParams(
            collective_id=0, has_side_effects=True, vmem_limit_bytes=56 * 1024 * 1024
        ),
    )(
        residues, chain_ids[None, :], residue_valid[None, :], layer_weights, resampler_weights,
        norm_gains, norm_biases, latents, *tables
    )


def solution(mesh):
    placed = (
        P(("dp", "ctx"), None),
        P(("dp", "ctx")),
        P(("dp", "ctx")),
        P(None, "ctx", "tensor"),
        P(None, "ctx", "tensor"),
        P(),
        P(),
        P(),
    )
    return jax.shard_map(
        per_device,
        mesh=mesh,
        in_specs=placed,
        out_specs=(P(("dp", "ctx"), "tensor"), P(("dp", "ctx"), "tensor")),
        check_vma=False,
    )
```

time: 654 us -> 100 us (0.15)
  waiting for transfers between devices: 466 us -> 0 us
  Pallas kernels: 0 us -> 97.5 us
  blocking collectives: 92.8 us -> 0 us
  local copies, waits for them, and re-layouts: 40.7 us -> 2.2 us
  matrix products: 23.8 us -> 0 us
  other arithmetic: 13.9 us -> 0 us
  between operations: 14.4 us -> 0.65 us
    all_gather x5 -> x0, waiting for transfers between devices: 396 us -> none  [the longest x1 134 us: per_device(): lax.all_gather(layer_weights, 'ctx', axis=1, tiled=True)]
    pallas_call x0 -> x1, Pallas kernels: none -> 97.5 us  [per_device(): pl.pallas_call(kernel, out_shape=(jax.ShapeDtypeStruct((ROWS, SLICE), BF1...]
    all_gather x3 -> x0, blocking collectives: 92.8 us -> none  [the longest x2 63.3 us: combined_all(): pieces = jax.tree.map(lambda part: lax.all_gather(part, axis), value)]
    psum x1 -> x0, waiting for transfers between devices: 47.6 us -> none  [per_device(): summed = lax.psum(head_terms, 'tensor')]
    dynamic_slice x43 -> x0, local copies, waits for them, and re-layouts: 25.9 us -> none  [the longest x30 16.7 us: combined_all(): lax.scan(lambda total, piece: (join(total, piece), None), head, tail)]
    dot_general x18 -> x0, matrix products: 23.8 us -> none  [the longest x2 5.59 us: contract_last(): lax.dot_general(left, right, (((1,), (1,)), ((), ())), preferred_element_...]
    unnamed x8 -> x0, waiting for transfers between devices: 22.5 us -> none
  transfers between devices with their start and end apart: 7 -> 0, of which waited for: 7 -> 0; matrix products, arithmetic and copies ran while one was open for 4% -> 0% of each run, Pallas kernels for 0% -> 0%
where the time goes in v1:
time: 100 us
  Pallas kernels  97.5 us (98%)
  local copies, waits for them, and re-layouts  2.2 us (2%)
    pallas_call x1, Pallas kernels, per_device(): pl.pallas_call(kernel, out_shape=(jax.ShapeDtypeStruct((ROWS, SLICE), BF1...  97.5 us
    unnamed x4, local copies, waits for them, and re-layouts  2.2 us

profile of v1, /device:TPU:1, one launch (start us, length us, event | category | flops | bytes accessed | tf_op | source)
XLA Modules:
  0.0 100.3 jit_solution(15216272103272747495)
XLA Ops:
  0.6 97.5 %shard_map.131 = (bf16[128,640]{1,0:T(8,128)(2,1)}, bf16[8,640]{1,0:T(8,128)(2,1)}) custom-call(bf16[128,2560]{1,0:T(8,128)(2,1)} %res_ref.1, s32[1,128]{1,0:T(1,128)} %bitcast.2, s32[1,128]{1,0:T(1,128)} %bitcast.3, bf16[4,160,384]{2,1,0:T(8,128)(2,1)} %lw_ref.1, bf16[4,160,384]{2,1,0:T(8,128)(2,1)} %rw_ref.1, f32[3,2560]{1,0:T(4,128)} %gain_hbm.1, ...), custom_call_target="tpu_custom_call" | custom-call | tf_op jit(solution)/shard_map/pallas_call | solution.py:698
  98.1 0.0 copy-start
  98.1 1.6 %copy.16 = bf16[128,640]{1,0:T(8,128)(2,1)} copy(bf16[128,640]{1,0:T(8,128)(2,1)} %get-tuple-element.4) | data formatting | bytes 327680
  99.7 0.0 copy-done
  99.7 0.6 copy.17
Async XLA Ops:
  98.1 1.6 %copy-start = (bf16[8,640]{1,0:T(8,128)(2,1)S(1)}, bf16[8,640]{1,0:T(8,128)(2,1)}, u32[]{:S(2)}) copy-start(bf16[8,640]{1,0:T(8,128)(2,1)} %get-tuple-element.5) | copy-start | bytes 30724
